TPU v7x, 32 devices: a whole 2x2x4 slice. The times are simulated.
32 devices in a mesh: context: 16 (over z, y, x), tensor: 2 (over core).
Axes of the slice: x: 2, y: 2, z: 4, core: 2. Of those that a mesh axis runs over, the one named last changes fastest.
Arguments:
- query_proj: bfloat16 [2048, 8192], P('context', 'tensor'), may hold values from -6 to 6
- key_proj: bfloat16 [2048, 8192], P('context', 'tensor'), may hold values from -6 to 6
- value_proj: bfloat16 [2048, 8192], P('context', 'tensor'), may hold values from -6 to 6
- short_filter: float32 [3, 7, 8192], P(None, None, 'tensor'), may hold values from -2 to 2
- residues: float32 [16, 8192], P(None, 'tensor'), may hold values from -1.5 to 1.5
- decay: float32 [16, 8192], P(None, 'tensor'), may hold values from 0.00048828125 to 0.033333335
- skip_gain: float32 [8192], P('tensor'), may hold values from -6 to 6
- residual: bfloat16 [2048, 8192], P('context', 'tensor'), may hold values from -50 to 50
- norm_gain: float32 [8192], P('tensor'), may hold values from 0.5 to 1.5
Outputs:
- mixed: bfloat16 [2048, 8192], P('context', 'tensor')
- normed: bfloat16 [2048, 8192], P('context', 'tensor')
All inputs are finite; a program needn't handle non-finite values.
Results may differ from a plain program's by a relative error of at most 0.014.
Values may be sent and summed in bfloat16 or wider, within the bound.
A program may use at most 128 MiB of HBM per device.

v0:
```python
import functools

import jax
import jax.numpy as jnp
from jax import lax
from jax.experimental import pallas as pl
from jax.experimental.pallas import tpu as pltpu
from jax.sharding import PartitionSpec as P

MESH = pl.DeviceIdType.MESH
F32 = jnp.float32
BF16 = jnp.bfloat16


def kernel(
    count, peers, wire,
    q_ref, k_ref, v_ref, filter_ref, residue_ref, decay_ref, skip_ref, residual_ref, gain_ref,
    mixed_ref, normed_ref,
    rows_x, taps, modes, pole, weight, prod, gate, local, mix, total,
    state, prefix, plane,
    halo_out, halo_in, x_out, x_in, y_out, y_in, z_out, z_in, sq_out, sq_in,
    halo_ss, halo_rs, x_ss, x_rs, y_ss, y_rs, z_ss, z_rs, sq_ss, sq_rs,
):
    row_count, channels = q_ref.shape
    tap_count = filter_ref.shape[1]
    order = decay_ref.shape[0]
    tiles = channels // 128
    sub = min(8, tiles)
    groups = tiles // sub
    blocks = row_count // 8
    pitch = tiles * 8
    me = lax.axis_index("context")
    side = lax.axis_index("tensor")
    x = lax.rem(me, 2)
    y = lax.rem(me // 2, 2)
    z = me // 4
    depth = count // 4
    x_peer = me + 1 - 2 * x
    y_peer = me + 2 - 4 * y
    has_prev, has_next = me > 0, me < count - 1
    has_down, has_up = z > 0, z < depth - 1

    barrier = pltpu.get_barrier_semaphore()

    def greet(context, tensor):
        pl.semaphore_signal(barrier, inc=1, device_id=(context, tensor), device_id_type=MESH)

    greet(x_peer, side)
    greet(y_peer, side)
    for shift in range(1, peers):
        greet(me, lax.rem(side + shift, peers))
    pl.when(has_prev)(lambda: greet(me - 1, side))
    pl.when(has_next)(lambda: greet(me + 1, side))
    pl.when(has_down)(lambda: greet(me - 4, side))
    pl.when(has_up)(lambda: greet(me + 4, side))
    met = (
        1 + peers + has_prev.astype(jnp.int32) + has_next.astype(jnp.int32)
        + has_down.astype(jnp.int32) + has_up.astype(jnp.int32)
    )

    inputs = (q_ref, k_ref, v_ref)
    span = sub * 8
    for group in range(groups):
        for i in range(3):
            for l in range(sub):
                lane = (group * sub + l) * 128
                last = inputs[i][row_count - 16 : row_count, lane : lane + 128].astype(F32)
                mix[(i * sub + l) * 8 : (i * sub + l + 1) * 8, :] = last[8:16]
        halo_out[group] = mix[0 : 3 * span, :].astype(BF16)

    pl.semaphore_wait(barrier, met)

    def halo_copy(group):
        return pltpu.make_async_remote_copy(
            src_ref=halo_out.at[group], dst_ref=halo_in.at[group],
            send_sem=halo_ss.at[group], recv_sem=halo_rs.at[group],
            device_id=(lax.rem(me + 1, count), side), device_id_type=MESH,
        )

    def x_copy(group):
        return pltpu.make_async_remote_copy(
            src_ref=x_out.at[group], dst_ref=x_in.at[group],
            send_sem=x_ss.at[group], recv_sem=x_rs.at[group],
            device_id=(x_peer, side), device_id_type=MESH,
        )

    def y_copy(group):
        return pltpu.make_async_remote_copy(
            src_ref=y_out.at[group], dst_ref=y_in.at[group],
            send_sem=y_ss.at[group], recv_sem=y_rs.at[group],
            device_id=(y_peer, side), device_id_type=MESH,
        )

    def z_copy(group):
        return pltpu.make_async_remote_copy(
            src_ref=z_out.at[group], dst_ref=z_in.at[group],
            send_sem=z_ss.at[group], recv_sem=z_rs.at[group],
            device_id=(lax.rem(me + 4, count), side), device_id_type=MESH,
        )

    def to_wire(value):
        return value.reshape(order * sub, 128).astype(BF16) if wire == BF16 else value

    def from_wire(value):
        return value.astype(F32).reshape(order, sub, 128) if wire == BF16 else value

    @pl.when(has_next)
    def _():
        for group in range(groups):
            halo_copy(group).start()

    for l in range(tiles):
        lane = l * 128
        for i in range(3):
            base = (i * tiles + l) * 8
            taps[base : base + tap_count, :] = filter_ref[i, :, lane : lane + 128]
        for part in range(order // 8):
            base = (part * tiles + l) * 8
            modes[0, base : base + 8, :] = decay_ref[part * 8 : part * 8 + 8, lane : lane + 128]
            modes[1, base : base + 8, :] = residue_ref[part * 8 : part * 8 + 8, lane : lane + 128]
    for group in range(groups):
        for m in range(order):
            start = ((m // 8) * tiles + group * sub) * 8 + m % 8
            rate = modes[0, pl.ds(start, sub, stride=8), :]
            residue = modes[1, pl.ds(start, sub, stride=8), :]
            pole[group, 0, m] = jnp.exp(-rate)
            pole[group, 1, m] = jnp.exp(-rate * float(row_count))
            pole[group, 2, m] = jnp.exp(-rate * float(row_count - 8))
            weight[group, m] = residue * jnp.sqrt(1.0 - jnp.exp(-2.0 * rate))

    def convolve(i, group, block):
        first = group * sub * 8
        f = [
            taps[pl.ds(i * pitch + first + j, sub, stride=8), :] for j in range(tap_count)
        ]
        rows = []
        for s in range(1 - tap_count, 8):
            start = (block + (1 if s >= 0 else 0)) * pitch + first + s % 8
            rows.append(rows_x[i, pl.ds(start, sub, stride=8), :])
        outs = []
        for r in range(8):
            acc = rows[r + tap_count - 1] * f[0]
            for j in range(1, tap_count):
                acc = acc + rows[r + tap_count - 1 - j] * f[j]
            outs.append(acc)
        return outs

    def convert(group):
        def body(pair, carry):
            for i in range(3):
                for l in range(sub):
                    tile = group * sub + l
                    at = pl.ds(pl.multiple_of(pair * 16, 16), 16)
                    value = inputs[i][at, tile * 128 : tile * 128 + 128].astype(F32)
                    for half in range(2):
                        start = (pair * 2 + half + 1) * pitch + tile * 8
                        start = pl.multiple_of(start, 8)
                        rows_x[i, pl.ds(start, 8), :] = value[half * 8 : half * 8 + 8]
            return carry

        lax.fori_loop(0, blocks // 2, body, 0)

    def scan_block(group, block, h):
        keys = convolve(1, group, block)
        values = convolve(2, group, block)
        a = pole[group, 0]
        for r in range(8):
            p = keys[r] * values[r]
            prod[block * 8 + r, group] = p
            h = a * h + p[None]
        return h

    zero_state = jnp.zeros((order, sub, 128), F32)

    def phase_a(group):
        convert(group)
        h = lax.fori_loop(1, blocks, lambda b, h: scan_block(group, b, h), zero_state)
        state[group] = h

        @pl.when(has_prev)
        def _():
            halo_copy(group).wait_recv()
            for i in range(3):
                rows_x[i, group * span : group * span + span, :] = halo_in[
                    group, i * span : (i + 1) * span, :
                ].astype(F32)

        @pl.when(jnp.logical_not(has_prev))
        def _():
            for i in range(3):
                rows_x[i, group * span : group * span + span, :] = jnp.zeros((span, 128), F32)

        first = scan_block(group, 0, zero_state)
        e = state[group] + pole[group, 2] * first
        state[group] = e
        x_out[group] = to_wire(e)
        x_copy(group).start()

    def stage_y(group):
        x_copy(group).wait_recv()
        other = from_wire(x_in[group])
        own = state[group]
        b = pole[group, 1]
        upper = x.astype(F32)
        both = jnp.where(x == 1, b * other + own, b * own + other)
        prefix[group] = other * upper
        plane[group] = both
        y_out[group] = to_wire(both)
        y_copy(group).start()

    def stage_z(group):
        y_copy(group).wait_recv()
        other = from_wire(y_in[group])
        own = plane[group]
        b = pole[group, 1]
        b2 = b * b
        all4 = jnp.where(y == 1, b2 * other + own, b2 * own + other)
        plane[group] = all4
        here = prefix[group]
        prefix[group] = jnp.where(y == 1, here + jnp.where(x == 1, b, 1.0) * other, here)

        @pl.when(jnp.logical_and(z == 0, has_up))
        def _():
            z_out[group] = to_wire(all4)
            z_copy(group).start()

    def stage_chain(group):
        @pl.when(has_down)
        def _():
            z_copy(group).wait_recv()
            other = from_wire(z_in[group])
            b = pole[group, 1]
            b2 = b * b

            @pl.when(has_up)
            def _():
                z_out[group] = to_wire(b2 * b2 * other + plane[group])
                z_copy(group).start()

            scale = jnp.where(x == 1, b, 1.0) * jnp.where(y == 1, b2, 1.0)
            prefix[group] = prefix[group] + scale * other

    def phase_b(group):
        def body(block, h):
            gates = convolve(0, group, block)
            a = pole[group, 0]
            w = weight[group]
            skip = skip_ref[group]
            for r in range(8):
                p = prod[block * 8 + r, group]
                h = a * h + p[None]
                local[block * 8 + r, group] = jnp.sum(w * h, axis=0) + skip * p
                gate[block * 8 + r, group] = gates[r]
            return h

        lax.fori_loop(0, blocks, body, zero_state)

    def phase_c(group):
        def body(block, g):
            a = pole[group, 0]
            for r in range(8):
                g = a * g
                value = gate[block * 8 + r, group] * (
                    local[block * 8 + r, group] + jnp.sum(g, axis=0)
                )
                start = block * pitch + group * span + r
                mix[pl.ds(start, sub, stride=8), :] = value
            return g

        lax.fori_loop(0, blocks, body, weight[group] * prefix[group])

    for step in range(groups + 3):
        if step < groups:
            phase_a(step)
        if 0 <= step - 1 < groups:
            stage_y(step - 1)
        if 0 <= step - 2 < groups:
            stage_z(step - 2)
        if 0 <= step - 3 < groups:
            phase_b(step - 3)
            stage_chain(step - 3)
    for group in range(groups):
        phase_c(group)

    def finish(pair, carry):
        at = pl.ds(pl.multiple_of(pair * 16, 16), 16)
        squares = jnp.zeros((16, 128), F32)
        for l in range(tiles):
            parts = []
            for half in range(2):
                start = pl.multiple_of((pair * 2 + half) * pitch + l * 8, 8)
                parts.append(mix[pl.ds(start, 8), :])
            rounded = jnp.concatenate(parts, axis=0).astype(BF16)
            lanes = slice(l * 128, l * 128 + 128)
            mixed_ref[at, lanes] = rounded
            summed = residual_ref[at, lanes].astype(F32) + rounded.astype(F32)
            total[at, lanes] = summed
            squares = squares + summed * summed
        sq_out[at, :] = squares
        return carry

    lax.fori_loop(0, blocks // 2, finish, 0)

    def sq_copy(shift):
        return pltpu.make_async_remote_copy(
            src_ref=sq_out, dst_ref=sq_in.at[shift - 1],
            send_sem=sq_ss.at[shift - 1], recv_sem=sq_rs.at[shift - 1],
            device_id=(me, lax.rem(side + shift, peers)), device_id_type=MESH,
        )

    for shift in range(1, peers):
        sq_copy(shift).start()
    for shift in range(1, peers):
        sq_copy(shift).wait_recv()

    def normalise(pair, carry):
        at = pl.ds(pl.multiple_of(pair * 16, 16), 16)
        squares = sq_out[at, :]
        for shift in range(1, peers):
            squares = squares + sq_in[shift - 1, at, :]
        mean = jnp.sum(squares, axis=1, keepdims=True) / float(channels * peers)
        scale = lax.rsqrt(mean + 1e-05)
        for l in range(tiles):
            lanes = slice(l * 128, l * 128 + 128)
            normed_ref[at, lanes] = (total[at, lanes] * scale * gain_ref[:, lanes]).astype(BF16)
        return carry

    lax.fori_loop(0, blocks // 2, normalise, 0)

    for shift in range(1, peers):
        sq_copy(shift).wait_send()
    for group in range(groups):
        x_copy(group).wait_send()
        y_copy(group).wait_send()

    @pl.when(has_next)
    def _():
        for group in range(groups):
            halo_copy(group).wait_send()

    @pl.when(has_up)
    def _():
        for group in range(groups):
            z_copy(group).wait_send()


def shards(
    count, peers,
    query_proj, key_proj, value_proj, short_filter, residues, decay, skip_gain, residual, norm_gain
):
    rows, channels = query_proj.shape
    order = decay.shape[0]
    tiles = channels // 128
    sub = min(8, tiles)
    groups = tiles // sub
    wire = BF16 if sub == 8 else F32
    packet = (groups, order * sub, 128) if wire == BF16 else (groups, order, sub, 128)
    modal = (groups, order, sub, 128)
    by_row = pltpu.VMEM((rows, groups, sub, 128), F32)
    dma = pltpu.SemaphoreType.DMA
    whole = pl.BlockSpec(memory_space=pltpu.VMEM)
    out = jax.ShapeDtypeStruct((rows, channels), BF16)
    return pl.pallas_call(
        functools.partial(kernel, count, peers, wire),
        out_shape=(out, out),
        in_specs=[whole] * 9,
        out_specs=(whole, whole),
        scratch_shapes=[
            pltpu.VMEM((3, (rows + 8) * tiles, 128), F32),
            pltpu.VMEM((3 * tiles * 8, 128), F32),
            pltpu.VMEM((2, order * tiles, 128), F32),
            pltpu.VMEM((groups, 3, order, sub, 128), F32),
            pltpu.VMEM(modal, F32),
            by_row, by_row, by_row,
            pltpu.VMEM((rows * tiles, 128), F32),
            pltpu.VMEM((rows, channels), F32),
            pltpu.VMEM(modal, F32), pltpu.VMEM(modal, F32), pltpu.VMEM(modal, F32),
            pltpu.VMEM((groups, 3 * sub * 8, 128), BF16),
            pltpu.VMEM((groups, 3 * sub * 8, 128), BF16),
            pltpu.VMEM(packet, wire), pltpu.VMEM(packet, wire),
            pltpu.VMEM(packet, wire), pltpu.VMEM(packet, wire),
            pltpu.VMEM(packet, wire), pltpu.VMEM(packet, wire),
            pltpu.VMEM((rows, 128), F32), pltpu.VMEM((max(1, peers - 1), rows, 128), F32),
            dma((groups,)), dma((groups,)), dma((groups,)), dma((groups,)),
            dma((groups,)), dma((groups,)), dma((groups,)), dma((groups,)),
            dma((max(1, peers - 1),)), dma((max(1, peers - 1),)),
        ],
        compiler_params=pltpu.CompilerParams(
            collective_id=0, has_side_effects=True, vmem_limit_bytes=50 * 1024 * 1024
        ),
    )(
        query_proj, key_proj, value_proj, short_filter, residues, decay,
        skip_gain.reshape(groups, sub, 128), residual, norm_gain.reshape(1, channels),
    )


def solution(mesh):
    in_specs = (
        P("context", "tensor"),
        P("context", "tensor"),
        P("context", "tensor"),
        P(None, None, "tensor"),
        P(None, "tensor"),
        P(None, "tensor"),
        P("tensor"),
        P("context", "tensor"),
        P("tensor"),
    )
    out_specs = (P("context", "tensor"), P("context", "tensor"))
    return jax.shard_map(
        functools.partial(shards, mesh.shape["context"], mesh.shape["tensor"]),
        mesh=mesh, in_specs=in_specs, out_specs=out_specs, check_vma=False,
    )
```

profile of v0, /device:TPU:25, one launch (start us, length us, event | category | flops | bytes accessed | tf_op | source)
XLA Modules:
  0.0 43.8 jit_solution(6908638854688069080)
XLA Ops:
  0.6 0.0 copy-start
  0.6 1.2 %copy-done = bf16[128,4096]{1,0:T(8,128)(2,1)S(1)} copy-done((bf16[128,4096]{1,0:T(8,128)(2,1)S(1)}, bf16[128,4096]{1,0:T(8,128)(2,1)}, u32[]{:S(2)}) %copy-start) | copy-done | bytes 1048600
  1.9 0.0 copy-start.1
  1.9 1.0 %copy-done.1 = f32[3,7,4096]{2,1,0:T(8,128)S(1)} copy-done((f32[3,7,4096]{2,1,0:T(8,128)S(1)}, f32[3,7,4096]{2,1,0:T(8,128)}, u32[]{:S(2)}) %copy-start.1) | copy-done | bytes 344088
  2.9 0.0 copy-start.2
  2.9 0.9 %copy-done.2 = f32[16,4096]{1,0:T(8,128)S(1)} copy-done((f32[16,4096]{1,0:T(8,128)S(1)}, f32[16,4096]{1,0:T(8,128)}, u32[]{:S(2)}) %copy-start.2) | copy-done | bytes 262168
  3.8 0.0 copy-start.3
  3.8 0.9 %copy-done.3 = f32[16,4096]{1,0:T(8,128)S(1)} copy-done((f32[16,4096]{1,0:T(8,128)S(1)}, f32[16,4096]{1,0:T(8,128)}, u32[]{:S(2)}) %copy-start.3) | copy-done | bytes 262168
  4.8 0.0 copy-start.4
  4.8 0.7 %copy-done.4 = f32[4096]{0:T(1024)S(1)} copy-done((f32[4096]{0:T(1024)S(1)}, f32[4096]{0:T(1024)}, u32[]{:S(2)}) %copy-start.4) | copy-done | bytes 16408
  5.5 0.0 copy-start.5
  5.5 0.7 %copy-done.5 = f32[4096]{0:T(1024)S(1)} copy-done((f32[4096]{0:T(1024)S(1)}, f32[4096]{0:T(1024)}, u32[]{:S(2)}) %copy-start.5) | copy-done | bytes 16408
  6.2 35.6 %shard_map.104 = (bf16[128,4096]{1,0:T(8,128)(2,1)S(1)}, bf16[128,4096]{1,0:T(8,128)(2,1)S(1)}) custom-call(bf16[128,4096]{1,0:T(8,128)(2,1)S(1)} %copy-done, bf16[128,4096]{1,0:T(8,128)(2,1)} %k_ref.1, bf16[128,4096]{1,0:T(8,128)(2,1)} %v_ref.1, f32[3,7,4096]{2,1,0:T(8,128)S(1)} %copy-done.1, f32[16,4096]{1,0:T(8,128)S(1)} %copy-done.2, ...), custom_call_target="tpu_custom_call" | custom-call | tf_op jit(solution)/shard_map/pallas_call | solution.py:363
  41.8 1.0 %copy.13 = bf16[128,4096]{1,0:T(8,128)(2,1)} copy(bf16[128,4096]{1,0:T(8,128)(2,1)S(1)} %get-tuple-element.4) | data formatting | bytes 2097152
  42.8 1.0 %copy.14 = bf16[128,4096]{1,0:T(8,128)(2,1)} copy(bf16[128,4096]{1,0:T(8,128)(2,1)S(1)} %get-tuple-element.5) | data formatting | bytes 2097152
Async XLA Ops:
  0.6 1.2 %copy-start = (bf16[128,4096]{1,0:T(8,128)(2,1)S(1)}, bf16[128,4096]{1,0:T(8,128)(2,1)}, u32[]{:S(2)}) copy-start(bf16[128,4096]{1,0:T(8,128)(2,1)} %q_ref.1) | copy-start | bytes 3145732
  1.9 1.0 %copy-start.1 = (f32[3,7,4096]{2,1,0:T(8,128)S(1)}, f32[3,7,4096]{2,1,0:T(8,128)}, u32[]{:S(2)}) copy-start(f32[3,7,4096]{2,1,0:T(8,128)} %filter_ref.1) | copy-start | bytes 1032196
  2.9 0.9 %copy-start.2 = (f32[16,4096]{1,0:T(8,128)S(1)}, f32[16,4096]{1,0:T(8,128)}, u32[]{:S(2)}) copy-start(f32[16,4096]{1,0:T(8,128)} %residue_ref.1) | copy-start | bytes 786436
  3.8 0.9 %copy-start.3 = (f32[16,4096]{1,0:T(8,128)S(1)}, f32[16,4096]{1,0:T(8,128)}, u32[]{:S(2)}) copy-start(f32[16,4096]{1,0:T(8,128)} %decay_ref.1) | copy-start | bytes 786436
  4.8 0.7 %copy-start.4 = (f32[4096]{0:T(1024)S(1)}, f32[4096]{0:T(1024)}, u32[]{:S(2)}) copy-start(f32[4096]{0:T(1024)} %param.15) | copy-start | bytes 49156
  5.5 0.7 %copy-start.5 = (f32[4096]{0:T(1024)S(1)}, f32[4096]{0:T(1024)}, u32[]{:S(2)}) copy-start(f32[4096]{0:T(1024)} %param.17) | copy-start | bytes 49156
where the time goes:
time: 44.1 us; the launch traced here: 43.8 us
  Pallas kernels  35.6 us (81%)
  local copies, waits for them, and re-layouts  7.49 us (17%)
  between operations  0.66 us (1%)
    pallas_call x1, Pallas kernels, shards(): pl.pallas_call(functools.partial(kernel, count, peers, wire), out_shape=(...  35.6 us
    unnamed x14, local copies, waits for them, and re-layouts  7.49 us

commit v1 on v0

v1 whole, which is shorter than its diff:
```python
import functools

import jax
import jax.numpy as jnp
from jax import lax
from jax.experimental import pallas as pl
from jax.experimental.pallas import tpu as pltpu
from jax.sharding import PartitionSpec as P

MESH = pl.DeviceIdType.MESH
F32 = jnp.float32
BF16 = jnp.bfloat16


def kernel(
    count, peers, wire,
    q_hbm, k_hbm, v_hbm, filter_hbm, residue_hbm, decay_hbm, skip_hbm, residual_hbm, gain_hbm,
    mixed_ref, normed_ref,
    inputs, filter_ref, residue_ref, decay_ref, skip_ref, residual_ref, gain_ref, edge,
    rows_x, taps, modes, pole, weight, table, direct, prod, gate, starts, mix, total,
    state, first_ref, prefix, plane, column,
    halo_out, halo_in, x_out, x_in, y_out, y_in, z_out, z_in, sq_out, sq_in,
    in_sem, par_sem, edge_sem,
    halo_ss, halo_rs, x_ss, x_rs, y_ss, y_rs, z_ss, z_rs, sq_ss, sq_rs,
):
    row_count, channels = q_hbm.shape
    tap_count = filter_hbm.shape[1]
    order = decay_hbm.shape[0]
    tiles = channels // 128
    sub = min(8, tiles)
    groups = tiles // sub
    blocks = row_count // 8
    pitch = tiles * 8
    span = sub * 8
    me = lax.axis_index("context")
    side = lax.axis_index("tensor")
    x = lax.rem(me, 2)
    y = lax.rem(me // 2, 2)
    z = me // 4
    depth = count // 4
    x_peer = me + 1 - 2 * x
    y_peer = me + 2 - 4 * y
    has_prev, has_next = me > 0, me < count - 1

    sources = (q_hbm, k_hbm, v_hbm)

    def edge_copy(i):
        return pltpu.make_async_copy(
            sources[i].at[row_count - 16 : row_count], edge.at[i], edge_sem.at[i]
        )

    def input_copy(i, group):
        lanes = slice(group * sub * 128, (group + 1) * sub * 128)
        return pltpu.make_async_copy(
            sources[i].at[:, lanes], inputs.at[i, :, lanes], in_sem.at[i, group]
        )

    params = (
        (decay_hbm, decay_ref), (residue_hbm, residue_ref), (filter_hbm, filter_ref),
        (skip_hbm, skip_ref), (gain_hbm, gain_ref), (residual_hbm, residual_ref),
    )

    def param_copy(i):
        return pltpu.make_async_copy(params[i][0], params[i][1], par_sem.at[i])

    for i in range(3):
        edge_copy(i).start()
    for i in range(3):
        param_copy(i).start()
    for group in range(groups):
        input_copy(1, group).start()
        input_copy(2, group).start()
    for group in range(groups):
        input_copy(0, group).start()
    for i in range(3, 6):
        param_copy(i).start()

    barrier = pltpu.get_barrier_semaphore()

    def greet(context, tensor):
        pl.semaphore_signal(barrier, inc=1, device_id=(context, tensor), device_id_type=MESH)

    greet(x_peer, side)
    greet(y_peer, side)
    for shift in range(1, peers):
        greet(me, lax.rem(side + shift, peers))
    pl.when(has_prev)(lambda: greet(me - 1, side))
    pl.when(has_next)(lambda: greet(me + 1, side))
    for shift in range(1, depth):
        greet(lax.rem(me + 4 * shift, count), side)
    met = peers + depth + has_prev.astype(jnp.int32) + has_next.astype(jnp.int32)

    for i in range(3):
        edge_copy(i).wait()
    for group in range(groups):
        for i in range(3):
            for l in range(sub):
                lane = (group * sub + l) * 128
                last = edge[i, :, lane : lane + 128].astype(F32)
                mix[(i * sub + l) * 8 : (i * sub + l + 1) * 8, :] = last[8:16]
        halo_out[group] = mix[0 : 3 * span, :].astype(BF16)

    pl.semaphore_wait(barrier, met)

    def remote(src, dst, send, recv, context, tensor=side):
        return pltpu.make_async_remote_copy(
            src_ref=src, dst_ref=dst, send_sem=send, recv_sem=recv,
            device_id=(context, tensor), device_id_type=MESH,
        )

    def halo_copy(group):
        return remote(
            halo_out.at[group], halo_in.at[group], halo_ss.at[group], halo_rs.at[group],
            lax.rem(me + 1, count),
        )

    def x_copy(group):
        return remote(x_out.at[group], x_in.at[group], x_ss.at[group], x_rs.at[group], x_peer)

    def y_copy(group):
        return remote(y_out.at[group], y_in.at[group], y_ss.at[group], y_rs.at[group], y_peer)

    def z_copy(group, shift):
        return remote(
            z_out.at[group], z_in.at[group, shift - 1],
            z_ss.at[group, shift - 1], z_rs.at[group, shift - 1],
            lax.rem(me + 4 * shift, count),
        )

    def to_wire(value):
        return value.reshape(order * sub, 128).astype(BF16) if wire == BF16 else value

    def from_wire(value):
        return value.astype(F32).reshape(order, sub, 128) if wire == BF16 else value

    @pl.when(has_next)
    def _():
        for group in range(groups):
            halo_copy(group).start()

    for i in range(3):
        param_copy(i).wait()
    for l in range(tiles):
        lane = l * 128
        for i in range(3):
            base = (i * tiles + l) * 8
            taps[base : base + tap_count, :] = filter_ref[i, :, lane : lane + 128]
        for part in range(order // 8):
            base = (part * tiles + l) * 8
            modes[0, base : base + 8, :] = decay_ref[part * 8 : part * 8 + 8, lane : lane + 128]
            modes[1, base : base + 8, :] = residue_ref[part * 8 : part * 8 + 8, lane : lane + 128]
    for group in range(groups):
        for m in range(order):
            start = ((m // 8) * tiles + group * sub) * 8 + m % 8
            rate = modes[0, pl.ds(start, sub, stride=8), :]
            residue = modes[1, pl.ds(start, sub, stride=8), :]
            pole[group, 0, m] = jnp.exp(-rate)
            pole[group, 1, m] = jnp.exp(-rate * float(row_count))
            pole[group, 2, m] = jnp.exp(-rate * float(row_count - 8))
            pole[group, 3, m] = jnp.exp(-rate * 8.0)
            weight[group, m] = residue * jnp.sqrt(1.0 - jnp.exp(-2.0 * rate))

    def convolve(i, group, block):
        first = group * sub * 8
        f = [
            taps[pl.ds(i * pitch + first + j, sub, stride=8), :] for j in range(tap_count)
        ]
        rows = []
        for s in range(1 - tap_count, 8):
            start = (block + (1 if s >= 0 else 0)) * pitch + first + s % 8
            rows.append(rows_x[i, pl.ds(start, sub, stride=8), :])
        outs = []
        for r in range(8):
            acc = rows[r + tap_count - 1] * f[0]
            for j in range(1, tap_count):
                acc = acc + rows[r + tap_count - 1 - j] * f[j]
            outs.append(acc)
        return outs

    def convert(chosen, group):
        for i in chosen:
            input_copy(i, group).wait()

        def body(pair, carry):
            for i in chosen:
                for l in range(sub):
                    tile = group * sub + l
                    at = pl.ds(pl.multiple_of(pair * 16, 16), 16)
                    value = inputs[i, at, tile * 128 : tile * 128 + 128].astype(F32)
                    for half in range(2):
                        start = (pair * 2 + half + 1) * pitch + tile * 8
                        start = pl.multiple_of(start, 8)
                        rows_x[i, pl.ds(start, 8), :] = value[half * 8 : half * 8 + 8]
            return carry

        lax.fori_loop(0, blocks // 2, body, 0)

    def place_halo(chosen, group):
        at = slice(group * span, group * span + span)

        @pl.when(has_prev)
        def _():
            for i in chosen:
                rows_x[i, at, :] = halo_in[group, i * span : (i + 1) * span, :].astype(F32)

        @pl.when(jnp.logical_not(has_prev))
        def _():
            for i in chosen:
                rows_x[i, at, :] = jnp.zeros((span, 128), F32)

    def scan_block(group, block, h):
        keys = convolve(1, group, block)
        values = convolve(2, group, block)
        a = pole[group, 0]
        for r in range(8):
            p = keys[r] * values[r]
            prod[block * 8 + r, group] = p
            h = a * h + p[None]
        return h

    zero_state = jnp.zeros((order, sub, 128), F32)

    def phase_a(group):
        convert((1, 2), group)

        def body(block, h):
            starts[group, block] = h
            return scan_block(group, block, h)

        h = lax.fori_loop(1, blocks, body, zero_state)
        state[group] = h
        pl.when(has_prev)(lambda: halo_copy(group).wait_recv())
        place_halo((1, 2), group)
        first = scan_block(group, 0, zero_state)
        first_ref[group] = first
        e = state[group] + pole[group, 2] * first
        state[group] = e
        x_out[group] = to_wire(e)
        x_copy(group).start()

    def stage_y(group):
        x_copy(group).wait_recv()
        other = from_wire(x_in[group])
        own = state[group]
        b = pole[group, 1]
        both = jnp.where(x == 1, b * other + own, b * own + other)
        prefix[group] = other * x.astype(F32)
        plane[group] = both
        y_out[group] = to_wire(both)
        y_copy(group).start()

    def stage_z(group):
        y_copy(group).wait_recv()
        other = from_wire(y_in[group])
        own = plane[group]
        b = pole[group, 1]
        b2 = b * b
        all4 = jnp.where(y == 1, b2 * other + own, b2 * own + other)
        here = prefix[group]
        prefix[group] = jnp.where(y == 1, here + jnp.where(x == 1, b, 1.0) * other, here)
        z_out[group] = to_wire(all4)
        for shift in range(1, depth):
            pl.when(z + shift < depth)(lambda shift=shift: z_copy(group, shift).start())

    def stage_end(group):
        b = pole[group, 1]
        b2 = b * b
        b4 = b2 * b2
        column[...] = zero_state
        for shift in range(depth - 1, 0, -1):

            @pl.when(z >= shift)
            def _(shift=shift):
                z_copy(group, shift).wait_recv()
                column[...] = b4 * column[...] + from_wire(z_in[group, shift - 1])

        scale = jnp.where(x == 1, b, 1.0) * jnp.where(y == 1, b2, 1.0)
        prefix[group] = prefix[group] + scale * column[...]

    def phase_b(group):
        convert((0,), group)
        place_halo((0,), group)

        def body(block, carry):
            gates = convolve(0, group, block)
            for r in range(8):
                gate[block * 8 + r, group] = gates[r]
            return carry

        lax.fori_loop(0, blocks, body, 0)
        a = pole[group, 0]
        w = weight[group]
        direct[group, 0] = jnp.sum(w, axis=0) + skip_ref[group]
        for r in range(8):
            w = w * a
            table[group, r] = w
            if r < 7:
                direct[group, r + 1] = jnp.sum(w, axis=0)

    def phase_c(group):
        def emit(block, s):
            p = [prod[block * 8 + r, group] for r in range(8)]
            for r in range(8):
                value = jnp.sum(table[group, r] * s, axis=0)
                near = direct[group, 0] * p[r]
                for j in range(1, r + 1):
                    near = near + direct[group, j] * p[r - j]
                start = block * pitch + group * span + r
                mix[pl.ds(start, sub, stride=8), :] = gate[block * 8 + r, group] * (value + near)

        a8 = pole[group, 3]
        s = prefix[group]
        emit(0, s)

        def body(block, s):
            emit(block, s + starts[group, block])
            return pole[group, 3] * s

        lax.fori_loop(1, blocks, body, a8 * s + first_ref[group])

    for step in range(groups + 2):
        if step < groups:
            phase_a(step)
        if 0 <= step - 1 < groups:
            stage_y(step - 1)
        if 0 <= step - 2 < groups:
            stage_z(step - 2)
        if step == groups - 1:
            param_copy(3).wait()
            for group in range(0, groups, 3):
                phase_b(group)
        if step >= groups:
            for group in range(step - groups + 1, groups, 3):
                phase_b(group)
    for group in range(groups):
        stage_end(group)
        phase_c(group)

    param_copy(4).wait()
    param_copy(5).wait()

    def finish(pair, carry):
        at = pl.ds(pl.multiple_of(pair * 16, 16), 16)
        squares = jnp.zeros((16, 128), F32)
        for l in range(tiles):
            parts = []
            for half in range(2):
                start = pl.multiple_of((pair * 2 + half) * pitch + l * 8, 8)
                parts.append(mix[pl.ds(start, 8), :])
            rounded = jnp.concatenate(parts, axis=0).astype(BF16)
            lanes = slice(l * 128, l * 128 + 128)
            mixed_ref[at, lanes] = rounded
            summed = residual_ref[at, lanes].astype(F32) + rounded.astype(F32)
            total[at, lanes] = summed
            squares = squares + summed * summed
        sq_out[at, :] = squares
        return carry

    lax.fori_loop(0, blocks // 2, finish, 0)

    def sq_copy(shift):
        return remote(
            sq_out, sq_in.at[shift - 1], sq_ss.at[shift - 1], sq_rs.at[shift - 1],
            me, lax.rem(side + shift, peers),
        )

    for shift in range(1, peers):
        sq_copy(shift).start()
    for shift in range(1, peers):
        sq_copy(shift).wait_recv()

    def normalise(pair, carry):
        at = pl.ds(pl.multiple_of(pair * 16, 16), 16)
        squares = sq_out[at, :]
        for shift in range(1, peers):
            squares = squares + sq_in[shift - 1, at, :]
        mean = jnp.sum(squares, axis=1, keepdims=True) / float(channels * peers)
        scale = lax.rsqrt(mean + 1e-05)
        for l in range(tiles):
            lanes = slice(l * 128, l * 128 + 128)
            normed_ref[at, lanes] = (total[at, lanes] * scale * gain_ref[:, lanes]).astype(BF16)
        return carry

    lax.fori_loop(0, blocks // 2, normalise, 0)

    for shift in range(1, peers):
        sq_copy(shift).wait_send()
    for group in range(groups):
        x_copy(group).wait_send()
        y_copy(group).wait_send()
        for shift in range(1, depth):
            pl.when(z + shift < depth)(
                lambda group=group, shift=shift: z_copy(group, shift).wait_send()
            )

    @pl.when(has_next)
    def _():
        for group in range(groups):
            halo_copy(group).wait_send()


def shards(
    count, peers,
    query_proj, key_proj, value_proj, short_filter, residues, decay, skip_gain, residual, norm_gain
):
    rows, channels = query_proj.shape
    order = decay.shape[0]
    tap_count = short_filter.shape[1]
    tiles = channels // 128
    sub = min(8, tiles)
    groups = tiles // sub
    depth = count // 4
    wire = BF16 if sub == 8 else F32
    packet = (order * sub, 128) if wire == BF16 else (order, sub, 128)
    others = max(1, peers - 1)
    packets = pltpu.VMEM((groups, *packet), wire)
    modal = pltpu.VMEM((groups, order, sub, 128), F32)
    by_row = pltpu.VMEM((rows, groups, sub, 128), F32)
    dma = pltpu.SemaphoreType.DMA
    hbm = pl.BlockSpec(memory_space=pltpu.HBM)
    whole = pl.BlockSpec(memory_space=pltpu.VMEM)
    out = jax.ShapeDtypeStruct((rows, channels), BF16)
    return pl.pallas_call(
        functools.partial(kernel, count, peers, wire),
        out_shape=(out, out),
        in_specs=[hbm] * 9,
        out_specs=(whole, whole),
        scratch_shapes=[
            pltpu.VMEM((3, rows, channels), BF16),
            pltpu.VMEM((3, tap_count, channels), F32),
            pltpu.VMEM((order, channels), F32),
            pltpu.VMEM((order, channels), F32),
            pltpu.VMEM((groups, sub, 128), F32),
            pltpu.VMEM((rows, channels), BF16),
            pltpu.VMEM((1, channels), F32),
            pltpu.VMEM((3, 16, channels), BF16),
            pltpu.VMEM((3, (rows + 8) * tiles, 128), F32),
            pltpu.VMEM((3 * tiles * 8, 128), F32),
            pltpu.VMEM((2, order * tiles, 128), F32),
            pltpu.VMEM((groups, 4, order, sub, 128), F32),
            modal,
            pltpu.VMEM((groups, 8, order, sub, 128), F32),
            pltpu.VMEM((groups, 8, sub, 128), F32),
            by_row, by_row,
            pltpu.VMEM((groups, rows // 8, order, sub, 128), F32),
            pltpu.VMEM((rows * tiles, 128), F32),
            pltpu.VMEM((rows, channels), F32),
            modal, modal, modal, modal,
            pltpu.VMEM((order, sub, 128), F32),
            pltpu.VMEM((groups, 3 * sub * 8, 128), BF16),
            pltpu.VMEM((groups, 3 * sub * 8, 128), BF16),
            packets, packets, packets, packets, packets,
            pltpu.VMEM((groups, depth - 1, *packet), wire),
            pltpu.VMEM((rows, 128), F32), pltpu.VMEM((others, rows, 128), F32),
            dma((3, groups)), dma((6,)), dma((3,)),
            dma((groups,)), dma((groups,)), dma((groups,)), dma((groups,)),
            dma((groups,)), dma((groups,)), dma((groups, depth - 1)), dma((groups, depth - 1)),
            dma((others,)), dma((others,)),
        ],
        compiler_params=pltpu.CompilerParams(
            collective_id=0, has_side_effects=True, vmem_limit_bytes=60 * 1024 * 1024
        ),
    )(
        query_proj, key_proj, value_proj, short_filter, residues, decay,
        skip_gain.reshape(groups, sub, 128), residual, norm_gain.reshape(1, channels),
    )


def solution(mesh):
    in_specs = (
        P("context", "tensor"),
        P("context", "tensor"),
        P("context", "tensor"),
        P(None, None, "tensor"),
        P(None, "tensor"),
        P(None, "tensor"),
        P("tensor"),
        P("context", "tensor"),
        P("tensor"),
    )
    out_specs = (P("context", "tensor"), P("context", "tensor"))
    return jax.shard_map(
        functools.partial(shards, mesh.shape["context"], mesh.shape["tensor"]),
        mesh=mesh, in_specs=in_specs, out_specs=out_specs, check_vma=False,
    )
```

time: 44.1 us -> 35.4 us (0.80)
  Pallas kernels: 35.6 us -> 31 us
  local copies, waits for them, and re-layouts: 7.49 us -> 3.35 us
    pallas_call x1, Pallas kernels: 35.6 us -> 31 us  [shards(): pl.pallas_call(functools.partial(kernel, count, peers, wire), out_shape=(...]
    unnamed x14 -> x4, local copies, waits for them, and re-layouts: 7.49 us -> 3.35 us
where the time goes in v1:
time: 35.4 us; the launch traced here: 35 us
  Pallas kernels  31 us (88%)
  local copies, waits for them, and re-layouts  3.35 us (9%)
  between operations  0.65 us (2%)
    pallas_call x1, Pallas kernels, shards(): pl.pallas_call(functools.partial(kernel, count, peers, wire), out_shape=(...  31 us
    unnamed x4, local copies, waits for them, and re-layouts  3.35 us

profile of v1, /device:TPU:25, one launch (start us, length us, event | category | flops | bytes accessed | tf_op | source)
XLA Modules:
  0.0 35.0 jit_solution(687527814696819863)
XLA Ops:
  0.6 31.0 %shard_map.104 = (bf16[128,4096]{1,0:T(8,128)(2,1)}, bf16[128,4096]{1,0:T(8,128)(2,1)}) custom-call(bf16[128,4096]{1,0:T(8,128)(2,1)} %q_hbm.1, bf16[128,4096]{1,0:T(8,128)(2,1)} %k_hbm.1, bf16[128,4096]{1,0:T(8,128)(2,1)} %v_hbm.1, f32[3,7,4096]{2,1,0:T(8,128)} %filter_hbm.1, f32[16,4096]{1,0:T(8,128)} %residue_hbm.1, f32[16,4096]{1,0:T(8,128)} %decay_hbm.1, ...), custom_call_target="tpu_custom_call" | custom-call | tf_op jit(solution)/shard_map/pallas_call | solution.py:423
  31.6 0.0 copy-start
  31.6 2.4 %copy.13 = bf16[128,4096]{1,0:T(8,128)(2,1)} copy(bf16[128,4096]{1,0:T(8,128)(2,1)} %get-tuple-element.4) | data formatting | bytes 2097152
  34.0 0.0 copy-done
  34.0 1.0 %copy.14 = bf16[128,4096]{1,0:T(8,128)(2,1)} copy(bf16[128,4096]{1,0:T(8,128)(2,1)S(1)} %copy-done) | data formatting | bytes 2097152
Async XLA Ops:
  31.6 2.4 %copy-start = (bf16[128,4096]{1,0:T(8,128)(2,1)S(1)}, bf16[128,4096]{1,0:T(8,128)(2,1)}, u32[]{:S(2)}) copy-start(bf16[128,4096]{1,0:T(8,128)(2,1)} %get-tuple-element.5) | copy-start | bytes 3145732

commit v2 on v1

--- a/solution.py
+++ b/solution.py
@@ -14,13 +14,13 @@
 
 def kernel(
     count, peers, wire,
-    q_hbm, k_hbm, v_hbm, filter_hbm, residue_hbm, decay_hbm, skip_hbm, residual_hbm, gain_hbm,
-    mixed_ref, normed_ref,
-    inputs, filter_ref, residue_ref, decay_ref, skip_ref, residual_ref, gain_ref, edge,
-    rows_x, taps, modes, pole, weight, table, direct, prod, gate, starts, mix, total,
+    q_hbm, k_hbm, v_hbm, filter_hbm, residue_hbm, decay_hbm, skip_hbm, residual_hbm,
+    mixed_hbm, squares_ref,
+    inputs, filter_ref, residue_ref, decay_ref, skip_ref, residual_ref, edge,
+    rows_x, turn, taps, taps_raw, modes, pole, weight, table, direct, prod, gate, starts, mix, mixed,
     state, first_ref, prefix, plane, column,
     halo_out, halo_in, x_out, x_in, y_out, y_in, z_out, z_in, sq_out, sq_in,
-    in_sem, par_sem, edge_sem,
+    in_sem, par_sem, edge_sem, out_sem,
     halo_ss, halo_rs, x_ss, x_rs, y_ss, y_rs, z_ss, z_rs, sq_ss, sq_rs,
 ):
     row_count, channels = q_hbm.shape
@@ -57,7 +57,7 @@
 
     params = (
         (decay_hbm, decay_ref), (residue_hbm, residue_ref), (filter_hbm, filter_ref),
-        (skip_hbm, skip_ref), (gain_hbm, gain_ref), (residual_hbm, residual_ref),
+        (skip_hbm, skip_ref), (residual_hbm, residual_ref),
     )
 
     def param_copy(i):
@@ -72,7 +72,7 @@
         input_copy(2, group).start()
     for group in range(groups):
         input_copy(0, group).start()
-    for i in range(3, 6):
+    for i in range(3, 5):
         param_copy(i).start()
 
     barrier = pltpu.get_barrier_semaphore()
@@ -144,12 +144,16 @@
         lane = l * 128
         for i in range(3):
             base = (i * tiles + l) * 8
-            taps[base : base + tap_count, :] = filter_ref[i, :, lane : lane + 128]
+            taps_raw[base : base + tap_count, :] = filter_ref[i, :, lane : lane + 128]
         for part in range(order // 8):
             base = (part * tiles + l) * 8
             modes[0, base : base + 8, :] = decay_ref[part * 8 : part * 8 + 8, lane : lane + 128]
             modes[1, base : base + 8, :] = residue_ref[part * 8 : part * 8 + 8, lane : lane + 128]
     for group in range(groups):
+        for i in range(3):
+            for j in range(tap_count):
+                start = i * pitch + group * span + j
+                taps[group, i, j] = taps_raw[pl.ds(start, sub, stride=8), :]
         for m in range(order):
             start = ((m // 8) * tiles + group * sub) * 8 + m % 8
             rate = modes[0, pl.ds(start, sub, stride=8), :]
@@ -161,14 +165,8 @@
             weight[group, m] = residue * jnp.sqrt(1.0 - jnp.exp(-2.0 * rate))
 
     def convolve(i, group, block):
-        first = group * sub * 8
-        f = [
-            taps[pl.ds(i * pitch + first + j, sub, stride=8), :] for j in range(tap_count)
-        ]
-        rows = []
-        for s in range(1 - tap_count, 8):
-            start = (block + (1 if s >= 0 else 0)) * pitch + first + s % 8
-            rows.append(rows_x[i, pl.ds(start, sub, stride=8), :])
+        f = [taps[group, i, j] for j in range(tap_count)]
+        rows = [rows_x[i, group, block * 8 + 8 + r] for r in range(1 - tap_count, 8)]
         outs = []
         for r in range(8):
             acc = rows[r + tap_count - 1] * f[0]
@@ -182,31 +180,35 @@
             input_copy(i, group).wait()
 
         def body(pair, carry):
+            at = pl.ds(pl.multiple_of(pair * 16, 16), 16)
             for i in chosen:
                 for l in range(sub):
                     tile = group * sub + l
-                    at = pl.ds(pl.multiple_of(pair * 16, 16), 16)
                     value = inputs[i, at, tile * 128 : tile * 128 + 128].astype(F32)
                     for half in range(2):
-                        start = (pair * 2 + half + 1) * pitch + tile * 8
-                        start = pl.multiple_of(start, 8)
-                        rows_x[i, pl.ds(start, 8), :] = value[half * 8 : half * 8 + 8]
+                        start = half * span + l * 8
+                        turn[i, start : start + 8, :] = value[half * 8 : half * 8 + 8]
+            for i in chosen:
+                for r in range(16):
+                    start = (r // 8) * span + r % 8
+                    rows_x[i, group, pair * 16 + 8 + r] = turn[i, pl.ds(start, sub, stride=8), :]
             return carry
 
         lax.fori_loop(0, blocks // 2, body, 0)
 
     def place_halo(chosen, group):
-        at = slice(group * span, group * span + span)
-
         @pl.when(has_prev)
         def _():
             for i in chosen:
-                rows_x[i, at, :] = halo_in[group, i * span : (i + 1) * span, :].astype(F32)
+                turn[i, 0:span, :] = halo_in[group, i * span : (i + 1) * span, :].astype(F32)
+            for i in chosen:
+                for r in range(8):
+                    rows_x[i, group, r] = turn[i, pl.ds(r, sub, stride=8), :]
 
         @pl.when(jnp.logical_not(has_prev))
         def _():
             for i in chosen:
-                rows_x[i, at, :] = jnp.zeros((span, 128), F32)
+                rows_x[i, group, 0:8] = jnp.zeros((8, sub, 128), F32)
 
     def scan_block(group, block, h):
         keys = convolve(1, group, block)
@@ -337,7 +339,10 @@
         phase_c(group)
 
     param_copy(4).wait()
-    param_copy(5).wait()
+
+    def out_copy(pair):
+        at = pl.ds(pl.multiple_of(pair * 16, 16), 16)
+        return pltpu.make_async_copy(mixed.at[at], mixed_hbm.at[at], out_sem.at[pair])
 
     def finish(pair, carry):
         at = pl.ds(pl.multiple_of(pair * 16, 16), 16)
@@ -349,11 +354,11 @@
                 parts.append(mix[pl.ds(start, 8), :])
             rounded = jnp.concatenate(parts, axis=0).astype(BF16)
             lanes = slice(l * 128, l * 128 + 128)
-            mixed_ref[at, lanes] = rounded
+            mixed[at, lanes] = rounded
             summed = residual_ref[at, lanes].astype(F32) + rounded.astype(F32)
-            total[at, lanes] = summed
             squares = squares + summed * summed
         sq_out[at, :] = squares
+        out_copy(pair).start()
         return carry
 
     lax.fori_loop(0, blocks // 2, finish, 0)
@@ -369,20 +374,16 @@
     for shift in range(1, peers):
         sq_copy(shift).wait_recv()
 
-    def normalise(pair, carry):
-        at = pl.ds(pl.multiple_of(pair * 16, 16), 16)
-        squares = sq_out[at, :]
-        for shift in range(1, peers):
-            squares = squares + sq_in[shift - 1, at, :]
-        mean = jnp.sum(squares, axis=1, keepdims=True) / float(channels * peers)
-        scale = lax.rsqrt(mean + 1e-05)
-        for l in range(tiles):
-            lanes = slice(l * 128, l * 128 + 128)
-            normed_ref[at, lanes] = (total[at, lanes] * scale * gain_ref[:, lanes]).astype(BF16)
+    squares = sq_out[...]
+    for shift in range(1, peers):
+        squares = squares + sq_in[shift - 1]
+    squares_ref[...] = squares
+
+    def drain(pair, carry):
+        out_copy(pair).wait()
         return carry
 
-    lax.fori_loop(0, blocks // 2, normalise, 0)
-
+    lax.fori_loop(0, blocks // 2, drain, 0)
     for shift in range(1, peers):
         sq_copy(shift).wait_send()
     for group in range(groups):
@@ -397,6 +398,45 @@
     def _():
         for group in range(groups):
             halo_copy(group).wait_send()
+
+
+def normalise(
+    width, mixed_hbm, residual_hbm, squares_ref, gain_ref, out_hbm, normed_hbm,
+    mixed, residual, normed, mixed_sem, residual_sem, out_sem, normed_sem,
+):
+    row_count, channels = mixed_hbm.shape
+    tall = 32
+    pieces = row_count // tall
+
+    ends = (
+        (mixed_hbm, mixed, mixed_sem), (residual_hbm, residual, residual_sem),
+        (mixed, out_hbm, out_sem), (normed, normed_hbm, normed_sem),
+    )
+
+    def copy(kind, piece):
+        source, target, sems = ends[kind]
+        at = slice(piece * tall, piece * tall + tall)
+        return pltpu.make_async_copy(source.at[at], target.at[at], sems.at[piece])
+
+    for piece in range(pieces):
+        copy(0, piece).start()
+        copy(1, piece).start()
+    for piece in range(pieces):
+        copy(0, piece).wait()
+        copy(2, piece).start()
+        copy(1, piece).wait()
+        for part in range(tall // 16):
+            at = slice(piece * tall + part * 16, piece * tall + part * 16 + 16)
+            mean = jnp.sum(squares_ref[at, :], axis=1, keepdims=True) / float(width)
+            scale = lax.rsqrt(mean + 1e-05)
+            for l in range(channels // 128):
+                lanes = slice(l * 128, l * 128 + 128)
+                summed = residual[at, lanes].astype(F32) + mixed[at, lanes].astype(F32)
+                normed[at, lanes] = (summed * scale * gain_ref[:, lanes]).astype(BF16)
+        copy(3, piece).start()
+    for piece in range(pieces):
+        copy(2, piece).wait()
+        copy(3, piece).wait()
 
 
 def shards(
@@ -420,11 +460,11 @@
     hbm = pl.BlockSpec(memory_space=pltpu.HBM)
     whole = pl.BlockSpec(memory_space=pltpu.VMEM)
     out = jax.ShapeDtypeStruct((rows, channels), BF16)
-    return pl.pallas_call(
+    mixed, squares = pl.pallas_call(
         functools.partial(kernel, count, peers, wire),
-        out_shape=(out, out),
-        in_specs=[hbm] * 9,
-        out_specs=(whole, whole),
+        out_shape=(out, jax.ShapeDtypeStruct((rows, 128), F32)),
+        in_specs=[hbm] * 8,
+        out_specs=(hbm, whole),
         scratch_shapes=[
             pltpu.VMEM((3, rows, channels), BF16),
             pltpu.VMEM((3, tap_count, channels), F32),
@@ -432,9 +472,10 @@
             pltpu.VMEM((order, channels), F32),
             pltpu.VMEM((groups, sub, 128), F32),
             pltpu.VMEM((rows, channels), BF16),
-            pltpu.VMEM((1, channels), F32),
             pltpu.VMEM((3, 16, channels), BF16),
-            pltpu.VMEM((3, (rows + 8) * tiles, 128), F32),
+            pltpu.VMEM((3, groups, rows + 8, sub, 128), F32),
+            pltpu.VMEM((3, 16 * sub, 128), F32),
+            pltpu.VMEM((groups, 3, tap_count, sub, 128), F32),
             pltpu.VMEM((3 * tiles * 8, 128), F32),
             pltpu.VMEM((2, order * tiles, 128), F32),
             pltpu.VMEM((groups, 4, order, sub, 128), F32),
@@ -444,7 +485,7 @@
             by_row, by_row,
             pltpu.VMEM((groups, rows // 8, order, sub, 128), F32),
             pltpu.VMEM((rows * tiles, 128), F32),
-            pltpu.VMEM((rows, channels), F32),
+            pltpu.VMEM((rows, channels), BF16),
             modal, modal, modal, modal,
             pltpu.VMEM((order, sub, 128), F32),
             pltpu.VMEM((groups, 3 * sub * 8, 128), BF16),
@@ -452,7 +493,7 @@
             packets, packets, packets, packets, packets,
             pltpu.VMEM((groups, depth - 1, *packet), wire),
             pltpu.VMEM((rows, 128), F32), pltpu.VMEM((others, rows, 128), F32),
-            dma((3, groups)), dma((6,)), dma((3,)),
+            dma((3, groups)), dma((5,)), dma((3,)), dma((rows // 16,)),
             dma((groups,)), dma((groups,)), dma((groups,)), dma((groups,)),
             dma((groups,)), dma((groups,)), dma((groups, depth - 1)), dma((groups, depth - 1)),
             dma((others,)), dma((others,)),
@@ -462,8 +503,20 @@
         ),
     )(
         query_proj, key_proj, value_proj, short_filter, residues, decay,
-        skip_gain.reshape(groups, sub, 128), residual, norm_gain.reshape(1, channels),
+        skip_gain.reshape(groups, sub, 128), residual,
     )
+    pieces = rows // 32
+    block = pltpu.VMEM((rows, channels), BF16)
+    return pl.pallas_call(
+        functools.partial(normalise, channels * peers),
+        out_shape=(out, out),
+        in_specs=[hbm, hbm, whole, whole],
+        out_specs=(hbm, hbm),
+        scratch_shapes=[
+            block, block, block, dma((pieces,)), dma((pieces,)), dma((pieces,)), dma((pieces,))
+        ],
+        compiler_params=pltpu.CompilerParams(vmem_limit_bytes=60 * 1024 * 1024),
+    )(mixed, residual, squares, norm_gain.reshape(1, channels))
 
 
 def solution(mesh):

time: 35.4 us -> 34 us (0.960)
  local copies, waits for them, and re-layouts: 3.35 us -> 0 us
  Pallas kernels: 31 us -> 32.8 us
    pallas_call x0 -> x1, Pallas kernels: none -> 3.37 us  [shards(): pl.pallas_call(functools.partial(normalise, channels * peers), out_shape=...]
    unnamed x4 -> x0, local copies, waits for them, and re-layouts: 3.35 us -> none
    pallas_call x1, Pallas kernels: 31 us -> 29.5 us  [shards(): pl.pallas_call(functools.partial(kernel, count, peers, wire), out_shape=(...]
where the time goes in v2:
time: 34 us; the launch traced here: 33.5 us
  Pallas kernels  32.8 us (96%)
  between operations  0.64 us (2%)
    pallas_call x1, Pallas kernels, shards(): pl.pallas_call(functools.partial(kernel, count, peers, wire), out_shape=(...  29.5 us
    pallas_call x1, Pallas kernels, shards(): pl.pallas_call(functools.partial(normalise, channels * peers), out_shape=...  3.37 us

profile of v2, /device:TPU:25, one launch (start us, length us, event | category | flops | bytes accessed | tf_op | source)
XLA Modules:
  0.0 33.5 jit_solution(1910734479098897980)
XLA Ops:
  0.6 29.5 %shard_map.104 = (bf16[128,4096]{1,0:T(8,128)(2,1)}, f32[128,128]{1,0:T(8,128)}) custom-call(bf16[128,4096]{1,0:T(8,128)(2,1)} %q_hbm.1, bf16[128,4096]{1,0:T(8,128)(2,1)} %k_hbm.1, bf16[128,4096]{1,0:T(8,128)(2,1)} %v_hbm.1, f32[3,7,4096]{2,1,0:T(8,128)} %filter_hbm.1, f32[16,4096]{1,0:T(8,128)} %residue_hbm.1, f32[16,4096]{1,0:T(8,128)} %decay_hbm.1, ...), custom_call_target="tpu_custom_call" | custom-call | tf_op jit(solution)/shard_map/pallas_call | solution.py:463
  30.1 3.4 %shard_map.105 = (bf16[128,4096]{1,0:T(8,128)(2,1)}, bf16[128,4096]{1,0:T(8,128)(2,1)}) custom-call(bf16[128,4096]{1,0:T(8,128)(2,1)} %get-tuple-element.4.mixed_hbm, bf16[128,4096]{1,0:T(8,128)(2,1)} %residual_hbm.3, f32[128,128]{1,0:T(8,128)} %get-tuple-element.5.squares_ref, f32[1,4096]{1,0:T(1,128)} %bitcast.3), custom_call_target="tpu_custom_call" | custom-call | tf_op jit(solution)/shard_map/pallas_call | solution.py:510

commit v3 on v2

--- a/solution.py
+++ b/solution.py
@@ -50,7 +50,7 @@
         )
 
     def input_copy(i, group):
-        lanes = slice(group * sub * 128, (group + 1) * sub * 128)
+        lanes = pl.ds(pl.multiple_of(group * sub * 128, 128), sub * 128)
         return pltpu.make_async_copy(
             sources[i].at[:, lanes], inputs.at[i, :, lanes], in_sem.at[i, group]
         )
@@ -90,17 +90,12 @@
         greet(lax.rem(me + 4 * shift, count), side)
     met = peers + depth + has_prev.astype(jnp.int32) + has_next.astype(jnp.int32)
 
-    for i in range(3):
-        edge_copy(i).wait()
-    for group in range(groups):
-        for i in range(3):
-            for l in range(sub):
-                lane = (group * sub + l) * 128
-                last = edge[i, :, lane : lane + 128].astype(F32)
-                mix[(i * sub + l) * 8 : (i * sub + l + 1) * 8, :] = last[8:16]
-        halo_out[group] = mix[0 : 3 * span, :].astype(BF16)
-
-    pl.semaphore_wait(barrier, met)
+    def loop(low, high, step):
+        def body(index, carry):
+            step(index)
+            return carry
+
+        lax.fori_loop(low, high, body, 0)
 
     def remote(src, dst, send, recv, context, tensor=side):
         return pltpu.make_async_remote_copy(
@@ -133,23 +128,22 @@
     def from_wire(value):
         return value.astype(F32).reshape(order, sub, 128) if wire == BF16 else value
 
-    @pl.when(has_next)
-    def _():
-        for group in range(groups):
-            halo_copy(group).start()
-
     for i in range(3):
         param_copy(i).wait()
-    for l in range(tiles):
-        lane = l * 128
+
+    def spread(l):
+        lanes = pl.ds(pl.multiple_of(l * 128, 128), 128)
         for i in range(3):
-            base = (i * tiles + l) * 8
-            taps_raw[base : base + tap_count, :] = filter_ref[i, :, lane : lane + 128]
+            base = pl.multiple_of((i * tiles + l) * 8, 8)
+            taps_raw[pl.ds(base, tap_count), :] = filter_ref[i, :, lanes]
         for part in range(order // 8):
-            base = (part * tiles + l) * 8
-            modes[0, base : base + 8, :] = decay_ref[part * 8 : part * 8 + 8, lane : lane + 128]
-            modes[1, base : base + 8, :] = residue_ref[part * 8 : part * 8 + 8, lane : lane + 128]
-    for group in range(groups):
+            base = pl.multiple_of((part * tiles + l) * 8, 8)
+            modes[0, pl.ds(base, 8), :] = decay_ref[part * 8 : part * 8 + 8, lanes]
+            modes[1, pl.ds(base, 8), :] = residue_ref[part * 8 : part * 8 + 8, lanes]
+
+    loop(0, tiles, spread)
+
+    def prepare(group):
         for i in range(3):
             for j in range(tap_count):
                 start = i * pitch + group * span + j
@@ -164,6 +158,25 @@
             pole[group, 3, m] = jnp.exp(-rate * 8.0)
             weight[group, m] = residue * jnp.sqrt(1.0 - jnp.exp(-2.0 * rate))
 
+    loop(0, groups, prepare)
+    for i in range(3):
+        edge_copy(i).wait()
+
+    def pack(group):
+        for i in range(3):
+            for l in range(sub):
+                lanes = pl.ds(pl.multiple_of((group * sub + l) * 128, 128), 128)
+                last = edge[i, :, lanes].astype(F32)
+                mix[(i * sub + l) * 8 : (i * sub + l + 1) * 8, :] = last[8:16]
+        halo_out[group] = mix[0 : 3 * span, :].astype(BF16)
+
+    loop(0, groups, pack)
+    pl.semaphore_wait(barrier, met)
+
+    @pl.when(has_next)
+    def _():
+        loop(0, groups, lambda group: halo_copy(group).start())
+
     def convolve(i, group, block):
         f = [taps[group, i, j] for j in range(tap_count)]
         rows = [rows_x[i, group, block * 8 + 8 + r] for r in range(1 - tap_count, 8)]
@@ -184,7 +197,8 @@
             for i in chosen:
                 for l in range(sub):
                     tile = group * sub + l
-                    value = inputs[i, at, tile * 128 : tile * 128 + 128].astype(F32)
+                    lanes = pl.ds(pl.multiple_of(tile * 128, 128), 128)
+                    value = inputs[i, at, lanes].astype(F32)
                     for half in range(2):
                         start = half * span + l * 8
                         turn[i, start : start + 8, :] = value[half * 8 : half * 8 + 8]
@@ -320,24 +334,24 @@
 
         lax.fori_loop(1, blocks, body, a8 * s + first_ref[group])
 
-    for step in range(groups + 2):
-        if step < groups:
-            phase_a(step)
-        if 0 <= step - 1 < groups:
-            stage_y(step - 1)
-        if 0 <= step - 2 < groups:
-            stage_z(step - 2)
-        if step == groups - 1:
-            param_copy(3).wait()
-            for group in range(0, groups, 3):
-                phase_b(group)
-        if step >= groups:
-            for group in range(step - groups + 1, groups, 3):
-                phase_b(group)
-    for group in range(groups):
+    def forward(group):
+        phase_a(group)
+        pl.when(group >= 1)(lambda: stage_y(group - 1))
+        pl.when(group >= 2)(lambda: stage_z(group - 2))
+
+    def backward(group):
         stage_end(group)
         phase_c(group)
 
+    loop(0, groups, forward)
+    param_copy(3).wait()
+    loop(0, groups // 2, phase_b)
+    stage_y(groups - 1)
+    if groups >= 2:
+        stage_z(groups - 2)
+    loop(groups // 2, groups, phase_b)
+    stage_z(groups - 1)
+    loop(0, groups, backward)
     param_copy(4).wait()
 
     def out_copy(pair):
@@ -386,26 +400,23 @@
     lax.fori_loop(0, blocks // 2, drain, 0)
     for shift in range(1, peers):
         sq_copy(shift).wait_send()
-    for group in range(groups):
+
+    def settle(group):
         x_copy(group).wait_send()
         y_copy(group).wait_send()
         for shift in range(1, depth):
-            pl.when(z + shift < depth)(
-                lambda group=group, shift=shift: z_copy(group, shift).wait_send()
-            )
-
-    @pl.when(has_next)
-    def _():
-        for group in range(groups):
-            halo_copy(group).wait_send()
+            pl.when(z + shift < depth)(lambda shift=shift: z_copy(group, shift).wait_send())
+        pl.when(has_next)(lambda: halo_copy(group).wait_send())
+
+    loop(0, groups, settle)
 
 
 def normalise(
     width, mixed_hbm, residual_hbm, squares_ref, gain_ref, out_hbm, normed_hbm,
-    mixed, residual, normed, mixed_sem, residual_sem, out_sem, normed_sem,
+    mixed, residual, normed, scale_ref, mixed_sem, residual_sem, out_sem, normed_sem,
 ):
     row_count, channels = mixed_hbm.shape
-    tall = 32
+    tall = 16
     pieces = row_count // tall
 
     ends = (
@@ -415,28 +426,43 @@
 
     def copy(kind, piece):
         source, target, sems = ends[kind]
-        at = slice(piece * tall, piece * tall + tall)
+        at = pl.ds(pl.multiple_of(piece * tall, tall), tall)
         return pltpu.make_async_copy(source.at[at], target.at[at], sems.at[piece])
 
-    for piece in range(pieces):
+    def loop(step):
+        def body(index, carry):
+            step(index)
+            return carry
+
+        lax.fori_loop(0, pieces, body, 0)
+
+    def fetch(piece):
         copy(0, piece).start()
         copy(1, piece).start()
-    for piece in range(pieces):
+
+    loop(fetch)
+    mean = jnp.sum(squares_ref[...], axis=1, keepdims=True) / float(width)
+    scale_ref[...] = jnp.broadcast_to(lax.rsqrt(mean + 1e-05), (row_count, 128))
+
+    def work(piece):
         copy(0, piece).wait()
         copy(2, piece).start()
         copy(1, piece).wait()
-        for part in range(tall // 16):
-            at = slice(piece * tall + part * 16, piece * tall + part * 16 + 16)
-            mean = jnp.sum(squares_ref[at, :], axis=1, keepdims=True) / float(width)
-            scale = lax.rsqrt(mean + 1e-05)
-            for l in range(channels // 128):
-                lanes = slice(l * 128, l * 128 + 128)
-                summed = residual[at, lanes].astype(F32) + mixed[at, lanes].astype(F32)
-                normed[at, lanes] = (summed * scale * gain_ref[:, lanes]).astype(BF16)
+        at = pl.ds(pl.multiple_of(piece * tall, tall), tall)
+        scale = scale_ref[at, :]
+        for l in range(channels // 128):
+            lanes = slice(l * 128, l * 128 + 128)
+            summed = residual[at, lanes].astype(F32) + mixed[at, lanes].astype(F32)
+            normed[at, lanes] = (summed * scale * gain_ref[:, lanes]).astype(BF16)
         copy(3, piece).start()
-    for piece in range(pieces):
+
+    loop(work)
+
+    def drain(piece):
         copy(2, piece).wait()
         copy(3, piece).wait()
+
+    loop(drain)
 
 
 def shards(
@@ -505,7 +531,7 @@
         query_proj, key_proj, value_proj, short_filter, residues, decay,
         skip_gain.reshape(groups, sub, 128), residual,
     )
-    pieces = rows // 32
+    pieces = rows // 16
     block = pltpu.VMEM((rows, channels), BF16)
     return pl.pallas_call(
         functools.partial(normalise, channels * peers),
@@ -513,7 +539,7 @@
         in_specs=[hbm, hbm, whole, whole],
         out_specs=(hbm, hbm),
         scratch_shapes=[
-            block, block, block, dma((pieces,)), dma((pieces,)), dma((pieces,)), dma((pieces,))
+            block, block, block, pltpu.VMEM((rows, 128), F32), dma((pieces,)), dma((pieces,)), dma((pieces,)), dma((pieces,))
         ],
         compiler_params=pltpu.CompilerParams(vmem_limit_bytes=60 * 1024 * 1024),
     )(mixed, residual, squares, norm_gain.reshape(1, channels))

time: 34 us -> 34.1 us (level)
  Pallas kernels: 32.8 us -> 33.2 us
where the time goes in v3:
time: 34.1 us; the launch traced here: 33.8 us
  Pallas kernels  33.2 us (97%)
  between operations  0.64 us (2%)
    pallas_call x1, Pallas kernels, shards(): pl.pallas_call(functools.partial(kernel, count, peers, wire), out_shape=(...  29.7 us
    pallas_call x1, Pallas kernels, shards(): pl.pallas_call(functools.partial(normalise, channels * peers), out_shape=...  3.46 us

profile of v3, /device:TPU:25, one launch (start us, length us, event | category | flops | bytes accessed | tf_op | source)
XLA Modules:
  0.0 33.8 jit_solution(524467362696775885)
XLA Ops:
  0.6 29.7 %shard_map.104 = (bf16[128,4096]{1,0:T(8,128)(2,1)}, f32[128,128]{1,0:T(8,128)}) custom-call(bf16[128,4096]{1,0:T(8,128)(2,1)} %q_hbm.1, bf16[128,4096]{1,0:T(8,128)(2,1)} %k_hbm.1, bf16[128,4096]{1,0:T(8,128)(2,1)} %v_hbm.1, f32[3,7,4096]{2,1,0:T(8,128)} %filter_hbm.1, f32[16,4096]{1,0:T(8,128)} %residue_hbm.1, f32[16,4096]{1,0:T(8,128)} %decay_hbm.1, ...), custom_call_target="tpu_custom_call" | custom-call | tf_op jit(solution)/shard_map/pallas_call | solution.py:489
  30.3 3.5 %shard_map.105 = (bf16[128,4096]{1,0:T(8,128)(2,1)}, bf16[128,4096]{1,0:T(8,128)(2,1)}) custom-call(bf16[128,4096]{1,0:T(8,128)(2,1)} %get-tuple-element.4.mixed_hbm, bf16[128,4096]{1,0:T(8,128)(2,1)} %residual_hbm.3, f32[128,128]{1,0:T(8,128)} %get-tuple-element.5.squares_ref, f32[1,4096]{1,0:T(1,128)} %bitcast.3), custom_call_target="tpu_custom_call" | custom-call | tf_op jit(solution)/shard_map/pallas_call | solution.py:536

commit v4 on v3

--- a/solution.py
+++ b/solution.py
@@ -103,10 +103,11 @@
             device_id=(context, tensor), device_id_type=MESH,
         )
 
-    def halo_copy(group):
+    def halo_copy(group, part):
+        at = pl.ds(span, 2 * span) if part == 0 else pl.ds(0, span)
         return remote(
-            halo_out.at[group], halo_in.at[group], halo_ss.at[group], halo_rs.at[group],
-            lax.rem(me + 1, count),
+            halo_out.at[group, at], halo_in.at[group, at],
+            halo_ss.at[group, part], halo_rs.at[group, part], lax.rem(me + 1, count),
         )
 
     def x_copy(group):
@@ -175,7 +176,7 @@
 
     @pl.when(has_next)
     def _():
-        loop(0, groups, lambda group: halo_copy(group).start())
+        halo_copy(0, 0).start()
 
     def convolve(i, group, block):
         f = [taps[group, i, j] for j in range(tap_count)]
@@ -237,6 +238,10 @@
     zero_state = jnp.zeros((order, sub, 128), F32)
 
     def phase_a(group):
+        @pl.when(jnp.logical_and(has_next, group + 1 < groups))
+        def _():
+            halo_copy(group + 1, 0).start()
+
         convert((1, 2), group)
 
         def body(block, h):
@@ -245,7 +250,7 @@
 
         h = lax.fori_loop(1, blocks, body, zero_state)
         state[group] = h
-        pl.when(has_prev)(lambda: halo_copy(group).wait_recv())
+        pl.when(has_prev)(lambda: halo_copy(group, 0).wait_recv())
         place_halo((1, 2), group)
         first = scan_block(group, 0, zero_state)
         first_ref[group] = first
@@ -253,6 +258,7 @@
         state[group] = e
         x_out[group] = to_wire(e)
         x_copy(group).start()
+        pl.when(has_next)(lambda: halo_copy(group, 1).start())
 
     def stage_y(group):
         x_copy(group).wait_recv()
@@ -295,6 +301,7 @@
 
     def phase_b(group):
         convert((0,), group)
+        pl.when(has_prev)(lambda: halo_copy(group, 1).wait_recv())
         place_halo((0,), group)
 
         def body(block, carry):
@@ -406,14 +413,18 @@
         y_copy(group).wait_send()
         for shift in range(1, depth):
             pl.when(z + shift < depth)(lambda shift=shift: z_copy(group, shift).wait_send())
-        pl.when(has_next)(lambda: halo_copy(group).wait_send())
+
+        @pl.when(has_next)
+        def _():
+            halo_copy(group, 0).wait_send()
+            halo_copy(group, 1).wait_send()
 
     loop(0, groups, settle)
 
 
 def normalise(
-    width, mixed_hbm, residual_hbm, squares_ref, gain_ref, out_hbm, normed_hbm,
-    mixed, residual, normed, scale_ref, mixed_sem, residual_sem, out_sem, normed_sem,
+    width, mixed_hbm, residual_hbm, squares_hbm, gain_hbm, out_hbm, normed_hbm,
+    mixed, residual, normed, squares_ref, gain_ref, scale_ref, small_sem, mixed_sem, residual_sem, out_sem, normed_sem,
 ):
     row_count, channels = mixed_hbm.shape
     tall = 16
@@ -440,7 +451,15 @@
         copy(0, piece).start()
         copy(1, piece).start()
 
+    small = (
+        pltpu.make_async_copy(squares_hbm, squares_ref, small_sem.at[0]),
+        pltpu.make_async_copy(gain_hbm, gain_ref, small_sem.at[1]),
+    )
+    small[0].start()
+    small[1].start()
     loop(fetch)
+    small[0].wait()
+    small[1].wait()
     mean = jnp.sum(squares_ref[...], axis=1, keepdims=True) / float(width)
     scale_ref[...] = jnp.broadcast_to(lax.rsqrt(mean + 1e-05), (row_count, 128))
 
@@ -520,7 +539,7 @@
             pltpu.VMEM((groups, depth - 1, *packet), wire),
             pltpu.VMEM((rows, 128), F32), pltpu.VMEM((others, rows, 128), F32),
             dma((3, groups)), dma((5,)), dma((3,)), dma((rows // 16,)),
-            dma((groups,)), dma((groups,)), dma((groups,)), dma((groups,)),
+            dma((groups, 2)), dma((groups, 2)), dma((groups,)), dma((groups,)),
             dma((groups,)), dma((groups,)), dma((groups, depth - 1)), dma((groups, depth - 1)),
             dma((others,)), dma((others,)),
         ],
@@ -536,10 +555,11 @@
     return pl.pallas_call(
         functools.partial(normalise, channels * peers),
         out_shape=(out, out),
-        in_specs=[hbm, hbm, whole, whole],
+        in_specs=[hbm] * 4,
         out_specs=(hbm, hbm),
         scratch_shapes=[
-            block, block, block, pltpu.VMEM((rows, 128), F32), dma((pieces,)), dma((pieces,)), dma((pieces,)), dma((pieces,))
+            block, block, block, pltpu.VMEM((rows, 128), F32), pltpu.VMEM((1, channels), F32),
+            pltpu.VMEM((rows, 128), F32), dma((2,)), dma((pieces,)), dma((pieces,)), dma((pieces,)), dma((pieces,))
         ],
         compiler_params=pltpu.CompilerParams(vmem_limit_bytes=60 * 1024 * 1024),
     )(mixed, residual, squares, norm_gain.reshape(1, channels))

time: 34.1 us -> 32.9 us (0.965)
  the two profiles are of different devices: /device:TPU:25 before, /device:TPU:9 now
where the time goes in v4:
time: 32.9 us; the launch traced here: 32.8 us
  Pallas kernels  32.1 us (98%)
  between operations  0.64 us (2%)
    pallas_call x1, Pallas kernels, shards(): pl.pallas_call(functools.partial(kernel, count, peers, wire), out_shape=(...  29.4 us
    pallas_call x1, Pallas kernels, shards(): pl.pallas_call(functools.partial(normalise, channels * peers), out_shape=...  2.69 us

profile of v4, /device:TPU:9, one launch (start us, length us, event | category | flops | bytes accessed | tf_op | source)
XLA Modules:
  0.0 32.8 jit_solution(4320231193166647274)
XLA Ops:
  0.6 29.4 %shard_map.104 = (bf16[128,4096]{1,0:T(8,128)(2,1)}, f32[128,128]{1,0:T(8,128)}) custom-call(bf16[128,4096]{1,0:T(8,128)(2,1)} %q_hbm.1, bf16[128,4096]{1,0:T(8,128)(2,1)} %k_hbm.1, bf16[128,4096]{1,0:T(8,128)(2,1)} %v_hbm.1, f32[3,7,4096]{2,1,0:T(8,128)} %filter_hbm.1, f32[16,4096]{1,0:T(8,128)} %residue_hbm.1, f32[16,4096]{1,0:T(8,128)} %decay_hbm.1, ...), custom_call_target="tpu_custom_call" | custom-call | tf_op jit(solution)/shard_map/pallas_call | solution.py:508
  30.1 2.7 %shard_map.105 = (bf16[128,4096]{1,0:T(8,128)(2,1)}, bf16[128,4096]{1,0:T(8,128)(2,1)}) custom-call(bf16[128,4096]{1,0:T(8,128)(2,1)} %get-tuple-element.4.mixed_hbm, bf16[128,4096]{1,0:T(8,128)(2,1)} %residual_hbm.3, f32[128,128]{1,0:T(8,128)} %get-tuple-element.5.squares_hbm, f32[1,4096]{1,0:T(1,128)} %bitcast.3), custom_call_target="tpu_custom_call" | custom-call | tf_op jit(solution)/shard_map/pallas_call | solution.py:555

commit v5 on v4

--- a/solution.py
+++ b/solution.py
@@ -18,7 +18,7 @@
     mixed_hbm, squares_ref,
     inputs, filter_ref, residue_ref, decay_ref, skip_ref, residual_ref, edge,
     rows_x, turn, taps, taps_raw, modes, pole, weight, table, direct, prod, gate, starts, mix, mixed,
-    state, first_ref, prefix, plane, column,
+    state, first_ref, prefix, plane,
     halo_out, halo_in, x_out, x_in, y_out, y_in, z_out, z_in, sq_out, sq_in,
     in_sem, par_sem, edge_sem, out_sem,
     halo_ss, halo_rs, x_ss, x_rs, y_ss, y_rs, z_ss, z_rs, sq_ss, sq_rs,
@@ -41,6 +41,7 @@
     x_peer = me + 1 - 2 * x
     y_peer = me + 2 - 4 * y
     has_prev, has_next = me > 0, me < count - 1
+    has_down, has_up = z > 0, z < depth - 1
 
     sources = (q_hbm, k_hbm, v_hbm)
 
@@ -86,9 +87,12 @@
         greet(me, lax.rem(side + shift, peers))
     pl.when(has_prev)(lambda: greet(me - 1, side))
     pl.when(has_next)(lambda: greet(me + 1, side))
-    for shift in range(1, depth):
-        greet(lax.rem(me + 4 * shift, count), side)
-    met = peers + depth + has_prev.astype(jnp.int32) + has_next.astype(jnp.int32)
+    pl.when(has_down)(lambda: greet(me - 4, side))
+    pl.when(has_up)(lambda: greet(me + 4, side))
+    met = (
+        1 + peers + has_prev.astype(jnp.int32) + has_next.astype(jnp.int32)
+        + has_down.astype(jnp.int32) + has_up.astype(jnp.int32)
+    )
 
     def loop(low, high, step):
         def body(index, carry):
@@ -116,11 +120,10 @@
     def y_copy(group):
         return remote(y_out.at[group], y_in.at[group], y_ss.at[group], y_rs.at[group], y_peer)
 
-    def z_copy(group, shift):
+    def z_copy(group):
         return remote(
-            z_out.at[group], z_in.at[group, shift - 1],
-            z_ss.at[group, shift - 1], z_rs.at[group, shift - 1],
-            lax.rem(me + 4 * shift, count),
+            z_out.at[group], z_in.at[group], z_ss.at[group], z_rs.at[group],
+            lax.rem(me + 4, count),
         )
 
     def to_wire(value):
@@ -280,24 +283,26 @@
         all4 = jnp.where(y == 1, b2 * other + own, b2 * own + other)
         here = prefix[group]
         prefix[group] = jnp.where(y == 1, here + jnp.where(x == 1, b, 1.0) * other, here)
-        z_out[group] = to_wire(all4)
-        for shift in range(1, depth):
-            pl.when(z + shift < depth)(lambda shift=shift: z_copy(group, shift).start())
+        plane[group] = all4
+
+        @pl.when(jnp.logical_and(z == 0, has_up))
+        def _():
+            z_out[group] = to_wire(all4)
+            z_copy(group).start()
 
     def stage_end(group):
+        z_copy(group).wait_recv()
+        other = from_wire(z_in[group])
         b = pole[group, 1]
         b2 = b * b
-        b4 = b2 * b2
-        column[...] = zero_state
-        for shift in range(depth - 1, 0, -1):
-
-            @pl.when(z >= shift)
-            def _(shift=shift):
-                z_copy(group, shift).wait_recv()
-                column[...] = b4 * column[...] + from_wire(z_in[group, shift - 1])
+
+        @pl.when(has_up)
+        def _():
+            z_out[group] = to_wire(b2 * b2 * other + plane[group])
+            z_copy(group).start()
 
         scale = jnp.where(x == 1, b, 1.0) * jnp.where(y == 1, b2, 1.0)
-        prefix[group] = prefix[group] + scale * column[...]
+        prefix[group] = prefix[group] + scale * other
 
     def phase_b(group):
         convert((0,), group)
@@ -346,19 +351,43 @@
         pl.when(group >= 1)(lambda: stage_y(group - 1))
         pl.when(group >= 2)(lambda: stage_z(group - 2))
 
-    def backward(group):
-        stage_end(group)
-        phase_c(group)
+    def end_at(turn_of, group):
+        @pl.when(z == turn_of if turn_of < 3 else z >= 3)
+        def _():
+            stage_end(group)
 
     loop(0, groups, forward)
     param_copy(3).wait()
-    loop(0, groups // 2, phase_b)
-    stage_y(groups - 1)
-    if groups >= 2:
-        stage_z(groups - 2)
-    loop(groups // 2, groups, phase_b)
-    stage_z(groups - 1)
-    loop(0, groups, backward)
+    if groups == 4:
+        end_at(1, 0)
+        loop(0, 2, phase_b)
+        stage_y(3)
+        stage_z(2)
+        end_at(1, 1)
+        end_at(2, 0)
+        loop(2, 4, phase_b)
+        stage_z(3)
+
+        def backward(group):
+            end_at(3, group)
+            pl.when(group < 3)(lambda: end_at(2, group + 1))
+            pl.when(group < 2)(lambda: end_at(1, group + 2))
+            phase_c(group)
+
+        loop(0, 4, backward)
+    else:
+        loop(0, groups, phase_b)
+        stage_y(groups - 1)
+        if groups >= 2:
+            stage_z(groups - 2)
+        stage_z(groups - 1)
+
+        def backward(group):
+            pl.when(has_down)(lambda: stage_end(group))
+            phase_c(group)
+
+        loop(0, groups, backward)
+
     param_copy(4).wait()
 
     def out_copy(pair):
@@ -411,8 +440,7 @@
     def settle(group):
         x_copy(group).wait_send()
         y_copy(group).wait_send()
-        for shift in range(1, depth):
-            pl.when(z + shift < depth)(lambda shift=shift: z_copy(group, shift).wait_send())
+        pl.when(has_up)(lambda: z_copy(group).wait_send())
 
         @pl.when(has_next)
         def _():
@@ -494,7 +522,6 @@
     tiles = channels // 128
     sub = min(8, tiles)
     groups = tiles // sub
-    depth = count // 4
     wire = BF16 if sub == 8 else F32
     packet = (order * sub, 128) if wire == BF16 else (order, sub, 128)
     others = max(1, peers - 1)
@@ -532,15 +559,13 @@
             pltpu.VMEM((rows * tiles, 128), F32),
             pltpu.VMEM((rows, channels), BF16),
             modal, modal, modal, modal,
-            pltpu.VMEM((order, sub, 128), F32),
             pltpu.VMEM((groups, 3 * sub * 8, 128), BF16),
             pltpu.VMEM((groups, 3 * sub * 8, 128), BF16),
-            packets, packets, packets, packets, packets,
-            pltpu.VMEM((groups, depth - 1, *packet), wire),
+            packets, packets, packets, packets, packets, packets,
             pltpu.VMEM((rows, 128), F32), pltpu.VMEM((others, rows, 128), F32),
             dma((3, groups)), dma((5,)), dma((3,)), dma((rows // 16,)),
             dma((groups, 2)), dma((groups, 2)), dma((groups,)), dma((groups,)),
-            dma((groups,)), dma((groups,)), dma((groups, depth - 1)), dma((groups, depth - 1)),
+            dma((groups,)), dma((groups,)), dma((groups,)), dma((groups,)),
             dma((others,)), dma((others,)),
         ],
         compiler_params=pltpu.CompilerParams(

time: 32.9 us -> 34.5 us (1.049)
  the two profiles are of different devices: /device:TPU:9 before, /device:TPU:25 now
where the time goes in v5:
time: 34.5 us; the launch traced here: 33.9 us
  Pallas kernels  33.3 us (97%)
  between operations  0.64 us (2%)
    pallas_call x1, Pallas kernels, shards(): pl.pallas_call(functools.partial(kernel, count, peers, wire), out_shape=(...  30.6 us
    pallas_call x1, Pallas kernels, shards(): pl.pallas_call(functools.partial(normalise, channels * peers), out_shape=...  2.69 us

profile of v5, /device:TPU:25, one launch (start us, length us, event | category | flops | bytes accessed | tf_op | source)
XLA Modules:
  0.0 33.9 jit_solution(899508783597204788)
XLA Ops:
  0.6 30.6 %shard_map.104 = (bf16[128,4096]{1,0:T(8,128)(2,1)}, f32[128,128]{1,0:T(8,128)}) custom-call(bf16[128,4096]{1,0:T(8,128)(2,1)} %q_hbm.1, bf16[128,4096]{1,0:T(8,128)(2,1)} %k_hbm.1, bf16[128,4096]{1,0:T(8,128)(2,1)} %v_hbm.1, f32[3,7,4096]{2,1,0:T(8,128)} %filter_hbm.1, f32[16,4096]{1,0:T(8,128)} %residue_hbm.1, f32[16,4096]{1,0:T(8,128)} %decay_hbm.1, ...), custom_call_target="tpu_custom_call" | custom-call | tf_op jit(solution)/shard_map/pallas_call | solution.py:535
  31.3 2.7 %shard_map.105 = (bf16[128,4096]{1,0:T(8,128)(2,1)}, bf16[128,4096]{1,0:T(8,128)(2,1)}) custom-call(bf16[128,4096]{1,0:T(8,128)(2,1)} %get-tuple-element.4.mixed_hbm, bf16[128,4096]{1,0:T(8,128)(2,1)} %residual_hbm.3, f32[128,128]{1,0:T(8,128)} %get-tuple-element.5.squares_hbm, f32[1,4096]{1,0:T(1,128)} %bitcast.3), custom_call_target="tpu_custom_call" | custom-call | tf_op jit(solution)/shard_map/pallas_call | solution.py:580

commit v6 on v4

--- a/solution.py
+++ b/solution.py
@@ -30,6 +30,7 @@
     sub = min(8, tiles)
     groups = tiles // sub
     blocks = row_count // 8
+    several = 3 if (blocks - 1) % 3 == 0 else 1
     pitch = tiles * 8
     span = sub * 8
     me = lax.axis_index("context")
@@ -244,11 +245,14 @@
 
         convert((1, 2), group)
 
-        def body(block, h):
-            starts[group, block] = h
-            return scan_block(group, block, h)
-
-        h = lax.fori_loop(1, blocks, body, zero_state)
+        def body(step, h):
+            for k in range(several):
+                block = 1 + step * several + k
+                starts[group, block] = h
+                h = scan_block(group, block, h)
+            return h
+
+        h = lax.fori_loop(0, (blocks - 1) // several, body, zero_state)
         state[group] = h
         pl.when(has_prev)(lambda: halo_copy(group, 0).wait_recv())
         place_halo((1, 2), group)
@@ -304,13 +308,15 @@
         pl.when(has_prev)(lambda: halo_copy(group, 1).wait_recv())
         place_halo((0,), group)
 
-        def body(block, carry):
-            gates = convolve(0, group, block)
-            for r in range(8):
-                gate[block * 8 + r, group] = gates[r]
+        def body(pair, carry):
+            for k in range(2):
+                block = pair * 2 + k
+                gates = convolve(0, group, block)
+                for r in range(8):
+                    gate[block * 8 + r, group] = gates[r]
             return carry
 
-        lax.fori_loop(0, blocks, body, 0)
+        lax.fori_loop(0, blocks // 2, body, 0)
         a = pole[group, 0]
         w = weight[group]
         direct[group, 0] = jnp.sum(w, axis=0) + skip_ref[group]
@@ -335,11 +341,14 @@
         s = prefix[group]
         emit(0, s)
 
-        def body(block, s):
-            emit(block, s + starts[group, block])
-            return pole[group, 3] * s
-
-        lax.fori_loop(1, blocks, body, a8 * s + first_ref[group])
+        def body(step, s):
+            for k in range(several):
+                block = 1 + step * several + k
+                emit(block, s + starts[group, block])
+                s = pole[group, 3] * s
+            return s
+
+        lax.fori_loop(0, (blocks - 1) // several, body, a8 * s + first_ref[group])
 
     def forward(group):
         phase_a(group)

time: 32.9 us -> 32.4 us (0.985)
  the two profiles are of different devices: /device:TPU:9 before, /device:TPU:25 now
where the time goes in v6:
time: 32.4 us; the launch traced here: 32 us
  Pallas kernels  31.3 us (97%)
  between operations  0.64 us (2%)
    pallas_call x1, Pallas kernels, shards(): pl.pallas_call(functools.partial(kernel, count, peers, wire), out_shape=(...  28.6 us
    pallas_call x1, Pallas kernels, shards(): pl.pallas_call(functools.partial(normalise, channels * peers), out_shape=...  2.69 us

profile of v6, /device:TPU:25, one launch (start us, length us, event | category | flops | bytes accessed | tf_op | source)
XLA Modules:
  0.0 32.0 jit_solution(7418411227436988205)
XLA Ops:
  0.6 28.6 %shard_map.104 = (bf16[128,4096]{1,0:T(8,128)(2,1)}, f32[128,128]{1,0:T(8,128)}) custom-call(bf16[128,4096]{1,0:T(8,128)(2,1)} %q_hbm.1, bf16[128,4096]{1,0:T(8,128)(2,1)} %k_hbm.1, bf16[128,4096]{1,0:T(8,128)(2,1)} %v_hbm.1, f32[3,7,4096]{2,1,0:T(8,128)} %filter_hbm.1, f32[16,4096]{1,0:T(8,128)} %residue_hbm.1, f32[16,4096]{1,0:T(8,128)} %decay_hbm.1, ...), custom_call_target="tpu_custom_call" | custom-call | tf_op jit(solution)/shard_map/pallas_call | solution.py:517
  29.3 2.7 %shard_map.105 = (bf16[128,4096]{1,0:T(8,128)(2,1)}, bf16[128,4096]{1,0:T(8,128)(2,1)}) custom-call(bf16[128,4096]{1,0:T(8,128)(2,1)} %get-tuple-element.4.mixed_hbm, bf16[128,4096]{1,0:T(8,128)(2,1)} %residual_hbm.3, f32[128,128]{1,0:T(8,128)} %get-tuple-element.5.squares_hbm, f32[1,4096]{1,0:T(1,128)} %bitcast.3), custom_call_target="tpu_custom_call" | custom-call | tf_op jit(solution)/shard_map/pallas_call | solution.py:564

commit v7 on v6

--- a/solution.py
+++ b/solution.py
@@ -30,7 +30,7 @@
     sub = min(8, tiles)
     groups = tiles // sub
     blocks = row_count // 8
-    several = 3 if (blocks - 1) % 3 == 0 else 1
+    several = 5 if (blocks - 1) % 5 == 0 else 1
     pitch = tiles * 8
     span = sub * 8
     me = lax.axis_index("context")

time: 32.4 us -> 32.2 us (level)
  no operation moved by 1% of the time
where the time goes in v7:
time: 32.2 us; the launch traced here: 31.9 us
  Pallas kernels  31.2 us (97%)
  between operations  0.64 us (2%)
    pallas_call x1, Pallas kernels, shards(): pl.pallas_call(functools.partial(kernel, count, peers, wire), out_shape=(...  28.5 us
    pallas_call x1, Pallas kernels, shards(): pl.pallas_call(functools.partial(normalise, channels * peers), out_shape=...  2.69 us

profile of v7, /device:TPU:25, one launch (start us, length us, event | category | flops | bytes accessed | tf_op | source)
XLA Modules:
  0.0 31.9 jit_solution(2428592468804571895)
XLA Ops:
  0.6 28.5 %shard_map.104 = (bf16[128,4096]{1,0:T(8,128)(2,1)}, f32[128,128]{1,0:T(8,128)}) custom-call(bf16[128,4096]{1,0:T(8,128)(2,1)} %q_hbm.1, bf16[128,4096]{1,0:T(8,128)(2,1)} %k_hbm.1, bf16[128,4096]{1,0:T(8,128)(2,1)} %v_hbm.1, f32[3,7,4096]{2,1,0:T(8,128)} %filter_hbm.1, f32[16,4096]{1,0:T(8,128)} %residue_hbm.1, f32[16,4096]{1,0:T(8,128)} %decay_hbm.1, ...), custom_call_target="tpu_custom_call" | custom-call | tf_op jit(solution)/shard_map/pallas_call | solution.py:517
  29.2 2.7 %shard_map.105 = (bf16[128,4096]{1,0:T(8,128)(2,1)}, bf16[128,4096]{1,0:T(8,128)(2,1)}) custom-call(bf16[128,4096]{1,0:T(8,128)(2,1)} %get-tuple-element.4.mixed_hbm, bf16[128,4096]{1,0:T(8,128)(2,1)} %residual_hbm.3, f32[128,128]{1,0:T(8,128)} %get-tuple-element.5.squares_hbm, f32[1,4096]{1,0:T(1,128)} %bitcast.3), custom_call_target="tpu_custom_call" | custom-call | tf_op jit(solution)/shard_map/pallas_call | solution.py:564
